TPU v7x, 32 devices: a whole 2x2x4 slice. The times are simulated.
32 devices in a mesh: col: 4 (over y, x), blk: 8 (over z, core).
Axes of the slice: x: 2, y: 2, z: 4, core: 2. Of those that a mesh axis runs over, the one named last changes fastest.
Arguments:
- corner_up: bfloat16 [4, 256, 256], P('col'), may hold values from -0.375 to 0.375
- corner_dn: bfloat16 [4, 256, 256], P('col'), may hold values from -0.375 to 0.375
- edge_top: bfloat16 [4, 256, 36, 256], P('col', 'blk'), may hold values from -6 to 6
- edge_bot: bfloat16 [4, 256, 36, 256], P('col', 'blk'), may hold values from -6 to 6
- edge_up: bfloat16 [4, 256, 36, 256], P('col', 'blk'), may hold values from -0.375 to 0.375
- edge_dn: bfloat16 [4, 256, 36, 256], P('col', 'blk'), may hold values from -0.375 to 0.375
- site_up: bfloat16 [4, 36, 36, 36, 36], P('col'), may hold values from -0.15625 to 0.15625
- site_dn: bfloat16 [4, 36, 36, 36, 36], P('col'), may hold values from -0.15625 to 0.15625
- proj_up: bfloat16 [4, 9216, 256], P('col', 'blk'), may hold values from -0.0625 to 0.0625
- proj_dn: bfloat16 [4, 9216, 256], P('col', 'blk'), may hold values from -0.0625 to 0.0625
Outputs:
- half_proj: bfloat16 [4, 9216, 256], P('col', 'blk')
- next_up: bfloat16 [4, 256, 256], P('col', 'blk')
- next_dn: bfloat16 [4, 256, 256], P('col', 'blk')
All inputs are finite; a program needn't handle non-finite values.
Results may differ from a plain program's by a relative error of at most 0.018.
Values may be sent and summed in bfloat16 or wider, within the bound.
No kernel may reach another device: no remote copies, remote signals or barrier semaphores. Data moves between devices by JAX's collectives and lax.ppermute only.
A program may use at most 128 MiB of HBM per device.

v0:
```python
import jax
import jax.numpy as jnp
from jax import lax
from jax.sharding import PartitionSpec as P


def from_behind(value, axis, steps):
    count = lax.axis_size(axis)
    pairs = [(source, (source + steps) % count) for source in range(count)]
    return lax.ppermute(value, axis, pairs)


def enlarge(edge, grown, site):
    rows, width, chi = edge.shape
    wide = jnp.dot(
        edge.reshape(rows * width, chi), grown, preferred_element_type=jnp.float32
    ).astype(jnp.bfloat16)
    wide = wide.reshape(rows, width * width, chi)
    table = site.transpose(2, 1, 3, 0).reshape(width * width, width * width)

    def one_row(slab):
        return jnp.dot(table, slab, preferred_element_type=jnp.float32).astype(jnp.bfloat16)

    block = lax.map(one_row, wide)
    return block.reshape(rows * width, width * chi)


def per_device(
    corner_up, corner_dn, edge_top, edge_bot, edge_up, edge_dn, site_up, site_dn, proj_up, proj_dn
):
    upper_c = corner_up[0]
    lower_c = corner_dn[0]
    chi = upper_c.shape[0]
    width = edge_top.shape[2]
    own_rows = edge_up.shape[1]
    pieces = (
        lax.all_gather(edge_top[0], "blk", axis=0, tiled=True),
        lax.all_gather(edge_bot[0], "blk", axis=0, tiled=True),
    )
    count = pieces[0].shape[0]
    first = jnp.dot(
        upper_c, pieces[0].reshape(count, width * chi), preferred_element_type=jnp.float32
    )
    second = jnp.dot(
        lower_c, pieces[1].reshape(count, width * chi), preferred_element_type=jnp.float32
    )
    grown_up = first
    grown_dn = second
    grown_up = grown_up.astype(jnp.bfloat16)
    grown_dn = grown_dn.astype(jnp.bfloat16)
    quad_up = enlarge(edge_up[0], grown_up, site_up[0])
    quad_dn = enlarge(edge_dn[0], grown_dn, site_dn[0])
    lower_p = proj_dn[0]
    upper_p = proj_up[0]
    contract = (((0,), (0,)), ((), ()))
    scale = 1.0 / (chi * width) ** 0.5
    cut_full = lax.psum(
        lax.dot_general(quad_dn, lower_p, contract, preferred_element_type=jnp.float32).astype(
            jnp.bfloat16
        ),
        "blk",
    )
    half = jnp.dot(quad_up, cut_full, preferred_element_type=jnp.float32)
    half_proj = (half * scale).astype(jnp.bfloat16)
    index = lax.axis_index("blk")
    own_up = lax.dynamic_slice_in_dim(grown_up, index * own_rows, own_rows, 0).reshape(
        own_rows * width, chi
    )
    own_dn = lax.dynamic_slice_in_dim(grown_dn, index * own_rows, own_rows, 0).reshape(
        own_rows * width, chi
    )
    first = lax.dot_general(upper_p, own_up, contract, preferred_element_type=jnp.float32)
    second = lax.dot_general(lower_p, own_dn, contract, preferred_element_type=jnp.float32)
    fresh = lax.psum_scatter(
        jnp.concatenate([first, second], axis=1).astype(jnp.bfloat16),
        "blk",
        scatter_dimension=0,
        tiled=True,
    )
    fresh_up = fresh[:, :chi]
    fresh_dn = fresh[:, chi:]
    moved_up, moved_dn = from_behind((fresh_up, fresh_dn), "col", 1)
    return (half_proj[None], moved_up[None], moved_dn[None])


def solution(mesh):
    in_specs = (
        P("col", None, None),
        P("col", None, None),
        P("col", "blk", None, None),
        P("col", "blk", None, None),
        P("col", "blk", None, None),
        P("col", "blk", None, None),
        P("col", None, None, None, None),
        P("col", None, None, None, None),
        P("col", "blk", None),
        P("col", "blk", None),
    )
    out_specs = (P("col", "blk", None), P("col", "blk", None), P("col", "blk", None))
    return jax.shard_map(
        per_device, mesh=mesh, in_specs=in_specs, out_specs=out_specs, check_vma=False
    )
```

profile of v0, /device:TPU:0, one launch (start us, length us, event | category | flops | bytes accessed | tf_op | source)
XLA Modules:
  0.0 700.7 jit_solution(2044784755267080769)
XLA Ops:
  10.2 21.0 %copy.34 = bf16[36,36,36,36]{3,2,1,0:T(8,128)(2,1)} copy(bf16[36,36,36,36]{2,0,1,3:T(8,128)(2,1)} %bitcast.80) | data formatting | bytes 6718464 | tf_op jit(solution)/shard_map/transpose | solution.py:19
  31.2 16.0 %reshape.42 = bf16[1296,1296]{1,0:T(8,128)(2,1)} reshape(bf16[36,36,36,36]{3,2,1,0:T(8,128)(2,1)} %copy.34) | data formatting | bytes 6718464 | tf_op jit(solution)/shard_map/reshape | solution.py:19
  47.7 21.0 %copy.30 = bf16[36,36,36,36]{3,2,1,0:T(8,128)(2,1)} copy(bf16[36,36,36,36]{2,0,1,3:T(8,128)(2,1)} %bitcast.81) | data formatting | bytes 6718464 | tf_op jit(solution)/shard_map/transpose | solution.py:19
  68.6 16.1 %reshape.38 = bf16[1296,1296]{1,0:T(8,128)(2,1)} reshape(bf16[36,36,36,36]{3,2,1,0:T(8,128)(2,1)} %copy.30) | data formatting | bytes 6718464 | tf_op jit(solution)/shard_map/reshape | solution.py:19
  84.8 6.6 copy.31
  91.4 6.0 convolution_convert_fusion.5
  97.4 18.8 %all-gather.5.cloned.1.call-done = bf16[1,256,36,256]{3,1,2,0:T(8,128)(2,1)} async-done(((bf16[1,32,36,256]{3,1,2,0:T(8,128)(2,1)}), bf16[1,256,36,256]{3,1,2,0:T(8,128)(2,1)}) %all-gather.5.cloned.1.call-update) | async-done | bytes 4718608 | tf_op jit(solution)/shard_map/all_gather | solution.py:37
  116.2 6.6 copy.27
  134.8 13.7 %fusion.11 = bf16[1152,9216]{0,1:T(8,128)(2,1)} fusion(bf16[256,9216]{1,0:T(8,128)(2,1)} %convolution_convert_fusion.5, bf16[1152,256]{1,0:T(8,128)(2,1)S(1)} %reshape_squeeze.7), kind=kOutput, calls=%fused_computation.15 | convolution fusion | flops 5446434816 | bytes 26542080 | tf_op jit(solution)/shard_map/dot_general | solution.py:15
  148.5 28.3 %copy.33 = bf16[1152,9216]{1,0:T(8,128)(2,1)} copy(bf16[1152,9216]{0,1:T(8,128)(2,1)} %fusion.11) | data formatting | bytes 42467328 | tf_op jit(solution)/shard_map/convert_element_type | solution.py:17
  176.9 42.1 %reshape.41 = bf16[32,1296,256]{2,1,0:T(8,128)(2,1)} reshape(bf16[1152,9216]{1,0:T(8,128)(2,1)} %copy.33) | data formatting | bytes 42467328 | tf_op jit(solution)/shard_map/reshape | solution.py:18
  218.9 7.3 %broadcast.3.clone.1 = bf16[32,1296,256]{2,1,0:T(8,128)(2,1)} broadcast(bf16[]{:T(256)} %constant.17.clone.1), dimensions={} | broadcast | bytes 21233666 | tf_op jit(solution)/shard_map/broadcast.1
  226.2 135.9 %while.21 = (s32[]{:T(128)}, bf16[32,1296,256]{2,1,0:T(8,128)(2,1)}, bf16[32,1296,256]{2,1,0:T(8,128)(2,1)}, bf16[1296,1296]{1,0:T(8,128)(2,1)}, s32[]{:T(128)}) while((s32[]{:T(128)}, bf16[32,1296,256]{2,1,0:T(8,128)(2,1)}, bf16[32,1296,256]{2,1,0:T(8,128)(2,1)}, bf16[1296,1296]{1,0:T(8,128)(2,1)}, s32[]{:T(128)}) %tuple.43), condition=%wide.region_3.4_spmd, body=%wide.region_2.3_spmd.sunk | while | flops 860295168 | bytes 4977725 | solution.py:24
  230.5 4.3 fusion.46
  247.4 4.3 fusion.46
  251.7 4.3 fusion.46
  307.0 4.3 fusion.46
  345.1 4.3 fusion.46
  362.1 37.0 %reshape.43 = bf16[1152,9216]{1,0:T(8,128)(2,1)} reshape(bf16[32,1296,256]{2,1,0:T(8,128)(2,1)} %get-tuple-element.48) | data formatting | bytes 42467328 | tf_op jit(solution)/shard_map/reshape | solution.py:25
  399.1 12.2 %convolution_convert_fusion.4 = bf16[9216,256]{1,0:T(8,128)(2,1)} fusion(bf16[1152,9216]{1,0:T(8,128)(2,1)} %reshape.43, bf16[1,1152,256]{2,1,0:T(8,128)(2,1)S(1)} %copy-done), kind=kOutput, calls=%fused_computation.16 | convolution fusion | flops 5438177280 | bytes 26542080 | tf_op jit(solution)/shard_map/dot_general | solution.py:58
  411.2 13.7 %fusion.10 = bf16[1152,9216]{0,1:T(8,128)(2,1)} fusion(bf16[256,9216]{1,0:T(8,128)(2,1)} %copy-done.2, bf16[1152,256]{1,0:T(8,128)(2,1)S(1)} %reshape_squeeze.6), kind=kOutput, calls=%fused_computation.14 | convolution fusion | flops 5446434816 | bytes 26542080 | tf_op jit(solution)/shard_map/dot_general | solution.py:15
  424.9 28.3 %copy.29 = bf16[1152,9216]{1,0:T(8,128)(2,1)} copy(bf16[1152,9216]{0,1:T(8,128)(2,1)} %fusion.10) | data formatting | bytes 42467328 | tf_op jit(solution)/shard_map/convert_element_type | solution.py:17
  453.2 42.1 %reshape.37 = bf16[32,1296,256]{2,1,0:T(8,128)(2,1)} reshape(bf16[1152,9216]{1,0:T(8,128)(2,1)} %copy.29) | data formatting | bytes 42467328 | tf_op jit(solution)/shard_map/reshape | solution.py:18
  499.4 7.3 %broadcast.3.clone = bf16[32,1296,256]{2,1,0:T(8,128)(2,1)} broadcast(bf16[]{:T(256)} %constant.17.clone.1), dimensions={} | broadcast | bytes 21233666 | tf_op jit(solution)/shard_map/broadcast.1
  506.7 137.0 %while.20 = (s32[]{:T(128)}, bf16[32,1296,256]{2,1,0:T(8,128)(2,1)}, bf16[32,1296,256]{2,1,0:T(8,128)(2,1)}, bf16[1296,1296]{1,0:T(8,128)(2,1)}, s32[]{:T(128)}) while((s32[]{:T(128)}, bf16[32,1296,256]{2,1,0:T(8,128)(2,1)}, bf16[32,1296,256]{2,1,0:T(8,128)(2,1)}, bf16[1296,1296]{1,0:T(8,128)(2,1)}, s32[]{:T(128)}) %tuple.40), condition=%wide.region_1.2_spmd, body=%wide.region_0.1_spmd.sunk | while | flops 860295168 | bytes 4977725 | solution.py:24
  506.7 4.3 fusion.43
  511.0 4.3 fusion.43
  515.3 4.3 fusion.43
  519.6 4.3 fusion.43
  523.9 4.3 fusion.43
  528.2 4.3 fusion.43
  532.5 4.4 fusion.43
  536.9 4.3 fusion.43
  541.1 4.3 fusion.43
  545.4 4.3 fusion.43
  553.9 4.5 fusion.43
  558.4 4.3 fusion.43
  562.7 4.3 fusion.43
  567.0 4.3 fusion.43
  571.3 4.3 fusion.43
  575.6 4.3 fusion.43
  579.9 4.3 fusion.43
  584.2 4.3 fusion.43
  588.5 4.3 fusion.43
  592.8 4.3 fusion.43
  626.7 4.3 fusion.43
  643.7 37.0 %reshape.39 = bf16[1152,9216]{1,0:T(8,128)(2,1)} reshape(bf16[32,1296,256]{2,1,0:T(8,128)(2,1)} %get-tuple-element.47) | data formatting | bytes 42467328 | tf_op jit(solution)/shard_map/reshape | solution.py:25
  682.1 12.1 %fusion.13 = bf16[1,1152,256]{2,1,0:T(8,128)(2,1)} fusion(bf16[1152,9216]{1,0:T(8,128)(2,1)} %reshape.39, bf16[9216,256]{1,0:T(8,128)(2,1)} %all-reduce.2.cloned.1.call-done), kind=kOutput, calls=%fused_computation.21 | convolution fusion | flops 5436407808 | bytes 26542080 | tf_op jit(solution)/shard_map/dot_general | solution.py:63
  (82 shorter events, 181.9 us)
Async XLA Ops:
  7.2 126.1 %copy-start = (bf16[1,1152,256]{2,1,0:T(8,128)(2,1)S(1)}, bf16[1,1152,256]{2,1,0:T(8,128)(2,1)}, u32[]{:S(2)}) copy-start(bf16[1,1152,256]{2,1,0:T(8,128)(2,1)} %param.23) | copy-start | bytes 1769476
  7.2 77.6 %all-gather.7.cloned.1.call-start = ((), (), s32[]{:S(2)}) async-start(), calls=%async_computation.3 | async-start | bytes 5308416 | tf_op jit(solution)/shard_map/all_gather | solution.py:38
  7.9 108.3 %all-gather.5.cloned.1.call-start = ((), (), s32[]{:S(2)}) async-start(), calls=%async_computation.2 | async-start | bytes 5308416 | tf_op jit(solution)/shard_map/all_gather | solution.py:37
  8.7 486.7 %reduce-scatter.4.cloned.1.call-start = ((), (), s32[]{:S(2)}) async-start(), calls=%async_computation.4 | async-start | bytes 294912
  31.2 16.0 %copy-start.3 = (bf16[1,32,36,256]{3,1,2,0:T(8,128)(2,1)S(1)}, bf16[1,32,36,256]{3,1,2,0:T(8,128)(2,1)}, u32[]{:S(2)}) copy-start(bf16[1,32,36,256]{3,1,2,0:T(8,128)(2,1)} %param.18) | copy-start | bytes 1769476
  68.6 22.8 %copy-start.4 = (bf16[1,256,256]{2,1,0:T(8,128)(2,1)S(1)}, bf16[1,256,256]{2,1,0:T(8,128)(2,1)}, u32[]{:S(2)}) copy-start(bf16[1,256,256]{2,1,0:T(8,128)(2,1)} %param.15) | copy-start | bytes 393220
  91.4 31.4 %copy-start.5 = (bf16[1,256,256]{2,1,0:T(8,128)(2,1)S(1)}, bf16[1,256,256]{2,1,0:T(8,128)(2,1)}, u32[]{:S(2)}) copy-start(bf16[1,256,256]{2,1,0:T(8,128)(2,1)} %param.14) | copy-start | bytes 393220
  126.6 2.2 copy-start.2
  134.6 547.5 %all-reduce.2.cloned.1.call-start = ((), (), s32[]{:S(2)}) async-start(), calls=%async_computation.1 | async-start | bytes 9437184 | tf_op jit(solution)/shard_map/psum | solution.py:57
  496.2 184.5 %collective-permute-start = (bf16[32,256]{0,1:T(8,128)(2,1)S(1)}, bf16[32,256]{0,1:T(8,128)(2,1)S(1)}, u32[]{:S(2)}, u32[]{:S(2)}) collective-permute-start(bf16[32,256]{0,1:T(8,128)(2,1)S(1)} %copy.39), channel_id=1, source_target_pairs={{0,8},{8,16},{16,24},{24,0},{1,9},{9,17},{17,25},{25,1},{2,10},{10... | collective-permute-start | bytes 49160 | tf_op jit(solution)/shard_map/ppermute | solution.py:10
  497.9 183.5 %collective-permute-start.1 = (bf16[32,256]{0,1:T(8,128)(2,1)S(1)}, bf16[32,256]{0,1:T(8,128)(2,1)S(1)}, u32[]{:S(2)}, u32[]{:S(2)}) collective-permute-start(bf16[32,256]{0,1:T(8,128)(2,1)S(1)} %copy.40), channel_id=1, source_target_pairs={{0,8},{8,16},{16,24},{24,0},{1,9},{9,17},{17,25},{25,1},{2,10},{10... | collective-permute-start | bytes 49160 | tf_op jit(solution)/shard_map/ppermute | solution.py:10
  682.1 12.1 %copy-start.1 = (bf16[1,1152,256]{2,1,0:T(8,128)(2,1)S(1)}, bf16[1,1152,256]{2,1,0:T(8,128)(2,1)}, u32[]{:S(2)}) copy-start(bf16[1,1152,256]{2,1,0:T(8,128)(2,1)} %param.23) | copy-start | bytes 1769476
Sparse Core Ops, SparseCore 0:
  9.6 54.3 all-gather.6
  65.6 50.5 all-gather.4
  134.7 29.1 reduce-scatter.3
  495.4 105.2 all-reduce.1
where the time goes:
time: 708 us; the launch traced here: 701 us
  matrix products  336 us (47%)
  local copies, waits for them, and re-layouts  327 us (46%)
  waiting for transfers between devices  20.2 us (3%)
  between operations  13.9 us (2%)
    dot_general x64, matrix products, one_row(): jnp.dot(table, slab, preferred_element_type=jnp.float32)  273 us
    reshape x2, local copies, waits for them, and re-layouts, enlarge(): wide = wide.reshape(rows, width * width, chi)  84.2 us
    reshape x2, local copies, waits for them, and re-layouts, enlarge(): return block.reshape(rows * width, width * chi)  73.9 us
    convert_element_type x2, local copies, waits for them, and re-layouts, enlarge(): wide = jnp.dot(edge.reshape(rows * width, chi), grown, preferred_element_...  56.7 us
    transpose x2, local copies, waits for them, and re-layouts, enlarge(): table = site.transpose(2, 1, 3, 0).reshape(width * width, width * width)  41.9 us
    reshape x2, local copies, waits for them, and re-layouts, enlarge(): table = site.transpose(2, 1, 3, 0).reshape(width * width, width * width)  32.2 us
    dot_general x2, matrix products, enlarge(): jnp.dot(edge.reshape(rows * width, chi), grown, preferred_element_type=jn...  27.4 us
    all_gather x1, waiting for transfers between devices, per_device(): lax.all_gather(edge_top[0], 'blk', axis=0, tiled=True)  18.8 us
  transfers between devices with their start and end apart: 6, of which 1 were waited for; matrix products, arithmetic and copies ran while one was open for 90% of the time, Pallas kernels for 0%

commit v1 on v0

v1 whole, which is shorter than its diff:
```python
import functools

import jax
import jax.numpy as jnp
from jax import lax
from jax.experimental import pallas as pl
from jax.experimental.pallas import tpu as pltpu
from jax.sharding import PartitionSpec as P

BF = jnp.bfloat16
F32 = jnp.float32
LANES = 128
VMEM = 56 * 1024 * 1024


def round_up(value, step):
    return (value + step - 1) // step * step


def params():
    return pltpu.CompilerParams(vmem_limit_bytes=VMEM)


def cost(flops, moved):
    return pl.CostEstimate(flops=int(flops), bytes_accessed=int(moved), transcendentals=0)


def table_kernel(width, vp, per, body, site_ref, out_ref):
    part = site_ref.shape[1]
    tail = width - body

    def one_group(g, carry):
        lane = pl.ds(pl.multiple_of(g * LANES, LANES), LANES)
        tails = []
        for t in range(part):
            pieces = []
            for r in range(per):
                pieces.append(site_ref[g * per + r, t].astype(F32))
                gap = vp - width if r < per - 1 else LANES - (per - 1) * vp - width
                pieces.append(jnp.zeros((width, gap), F32))
            full = jnp.concatenate(pieces, axis=1)
            out_ref[0, t * body : (t + 1) * body, lane] = full[:body].astype(BF)
            tails.append(full[body:])
        out_ref[0, part * body :, lane] = jnp.concatenate(tails, axis=0).astype(BF)
        return carry

    lax.fori_loop(0, width // per, one_group, 0)


def make_table(site, vp, per, body):
    width = site.shape[0]
    half = width // 2
    depth = width // per * LANES
    return pl.pallas_call(
        functools.partial(table_kernel, width, vp, per, body),
        grid=(2,),
        in_specs=[pl.BlockSpec((width, half, width, width), lambda h: (0, h, 0, 0))],
        out_specs=pl.BlockSpec((1, half * width, depth), lambda h: (h, 0, 0)),
        out_shape=jax.ShapeDtypeStruct((2, half * width, depth), BF),
        compiler_params=params(),
        cost_estimate=cost(0, 30e6),
        name="table",
    )(site)


def wide_kernel(vp, per, chunk, corner_ref, top_ref, edge_ref, grown_ref, wide_ref):
    legs = top_ref.shape[0]
    weights = []
    for q in range(legs // 2):
        right = jnp.concatenate([top_ref[2 * q], top_ref[2 * q + 1]], axis=1)
        g = jnp.dot(corner_ref[...], right, preferred_element_type=F32).astype(BF)
        grown_ref[q] = g
    pad = jnp.zeros((LANES - per * vp, LANES), F32)
    rows = edge_ref.shape[0] // vp

    def one_chunk(c, carry):
        left = edge_ref[pl.ds(pl.multiple_of(c * chunk * vp, 16), chunk * vp), :]
        res = [
            jnp.dot(left, grown_ref[q], preferred_element_type=F32) for q in range(legs // 2)
        ]
        for k in range(chunk):
            pieces = []
            for u in range(legs):
                lo = (u % 2) * LANES
                pieces.append(res[u // 2][k * vp : (k + 1) * vp, lo : lo + LANES])
                if u % per == per - 1:
                    pieces.append(pad)
            block = jnp.concatenate(pieces, axis=0).astype(BF)
            lo = (k % 2) * LANES
            wide_ref[c * (chunk // 2) + k // 2, :, lo : lo + LANES] = block
        return carry

    lax.fori_loop(0, rows // chunk, one_chunk, 0)


def make_wide(corner, top, edge, vp, per):
    width, chi, cols = top.shape
    legs = 2 * per
    steps = width // legs
    rows = edge.shape[0] // vp
    chunk = min(16, rows)
    depth = legs // per * LANES
    return pl.pallas_call(
        functools.partial(wide_kernel, vp, per, chunk),
        grid=(steps,),
        in_specs=[
            pl.BlockSpec((chi, chi), lambda s: (0, 0)),
            pl.BlockSpec((legs, chi, cols), lambda s: (s, 0, 0)),
            pl.BlockSpec(edge.shape, lambda s: (0, 0)),
        ],
        out_specs=[
            pl.BlockSpec((legs // 2, chi, 2 * cols), lambda s: (s, 0, 0)),
            pl.BlockSpec((rows // 2, depth, 2 * cols), lambda s: (0, s, 0)),
        ],
        out_shape=[
            jax.ShapeDtypeStruct((width // 2, chi, 2 * cols), BF),
            jax.ShapeDtypeStruct((rows // 2, steps * depth, 2 * cols), BF),
        ],
        compiler_params=params(),
        cost_estimate=cost(2 * rows * vp * chi * width * cols, 30e6),
        name="wide",
    )(corner, top, edge)


def place(res, pairs, body, vp, width, store):
    tail = width - body
    base = 2 * pairs * body
    keep = lax.broadcasted_iota(jnp.int32, (2 * tail, LANES), 0) < tail
    for p in range(pairs):
        for side in range(2):
            t = 2 * p + side
            pieces = []
            for i in range(2):
                lo = i * LANES
                pieces.append(res[t * body : (t + 1) * body, lo : lo + LANES])
                last = res[base + 2 * p * tail : base + 2 * (p + 1) * tail, lo : lo + LANES]
                if side:
                    last = pltpu.roll(last, tail, 0)
                pieces.append(jnp.where(keep, last, 0.0))
            store(p, side, jnp.concatenate(pieces, axis=0).astype(BF))


def cut_kernel(width, vp, body, table_ref, wide_ref, proj_ref, cut_ref, quad_ref):
    pairs = quad_ref.shape[0]
    step = pl.program_id(0)
    res = jnp.dot(table_ref[0], wide_ref[0], preferred_element_type=F32)
    at = pl.ds(pl.multiple_of(step * 2 * vp, 16), 2 * vp)

    def store(p, side, value):
        quad_ref[p, at, side * LANES : (side + 1) * LANES] = value

    place(res, pairs, body, vp, width, store)

    @pl.when(step == pl.num_programs(0) - 1)
    def _():
        for p in range(pairs):
            cut_ref[p] = jnp.dot(proj_ref[...], quad_ref[p], preferred_element_type=F32).astype(BF)


def make_cut(table, h, wide, proj_t, width, vp, body):
    count, depth, cols = wide.shape
    chi = proj_t.shape[0]
    pairs = width // 4
    rows = table.shape[1]
    return pl.pallas_call(
        functools.partial(cut_kernel, width, vp, body),
        grid=(count,),
        in_specs=[
            pl.BlockSpec((1, rows, depth), lambda s: (h, 0, 0)),
            pl.BlockSpec((1, depth, cols), lambda s: (s, 0, 0)),
            pl.BlockSpec(proj_t.shape, lambda s: (0, 0)),
        ],
        out_specs=pl.BlockSpec((pairs, chi, cols), lambda s: (0, 0, 0)),
        out_shape=jax.ShapeDtypeStruct((pairs, chi, cols), BF),
        scratch_shapes=[pltpu.VMEM((pairs, count * 2 * vp, cols), BF)],
        compiler_params=params(),
        cost_estimate=cost(2 * count * rows * depth * cols, 30e6),
        name="cut",
    )(table, wide, proj_t)


def quad_kernel(width, vp, body, table_ref, wide_ref, quad_ref):
    pairs = quad_ref.shape[0] // 2
    for h in range(2):
        res = jnp.dot(table_ref[h], wide_ref[0], preferred_element_type=F32)

        def store(p, side, value):
            quad_ref[h * pairs + p, :, side * LANES : (side + 1) * LANES] = value

        place(res, pairs, body, vp, width, store)


def make_quad(table, wide, width, vp, body):
    count, depth, cols = wide.shape
    pairs = width // 2
    return pl.pallas_call(
        functools.partial(quad_kernel, width, vp, body),
        grid=(count,),
        in_specs=[
            pl.BlockSpec(table.shape, lambda s: (0, 0, 0)),
            pl.BlockSpec((1, depth, cols), lambda s: (s, 0, 0)),
        ],
        out_specs=pl.BlockSpec((pairs, 2 * vp, cols), lambda s: (0, s, 0)),
        out_shape=jax.ShapeDtypeStruct((pairs, count * 2 * vp, cols), BF),
        compiler_params=params(),
        cost_estimate=cost(2 * count * width * width * depth * cols, 50e6),
        name="quad",
    )(table, wide)


def half_kernel(scale, quad_ref, first_ref, second_ref, out_ref):
    total = None
    pairs = first_ref.shape[0]
    for p in range(2 * pairs):
        right = first_ref[p] if p < pairs else second_ref[p - pairs]
        term = lax.dot_general(
            quad_ref[p], right, (((1,), (1,)), ((), ())), preferred_element_type=F32
        )
        total = term if total is None else total + term
    out_ref[...] = (total * scale).astype(out_ref.dtype)


def make_half(quad, cuts, begin, rows, dtype, scale):
    pairs, _, cols = quad.shape
    chi = cuts[0].shape[1]
    steps = 2
    block = rows // steps
    return pl.pallas_call(
        functools.partial(half_kernel, scale),
        grid=(steps,),
        in_specs=[
            pl.BlockSpec((pairs, block, cols), lambda s: (0, begin // block + s, 0)),
            pl.BlockSpec(cuts[0].shape, lambda s: (0, 0, 0)),
            pl.BlockSpec(cuts[1].shape, lambda s: (0, 0, 0)),
        ],
        out_specs=pl.BlockSpec((block, chi), lambda s: (s, 0)),
        out_shape=jax.ShapeDtypeStruct((rows, chi), dtype),
        compiler_params=params(),
        cost_estimate=cost(2 * rows * pairs * cols * chi, pairs * rows * cols * 2),
        name="half",
    )(quad, *cuts)


def per_device(
    corner_up, corner_dn, edge_top, edge_bot, edge_up, edge_dn, site_up, site_dn, proj_up, proj_dn
):
    count = lax.axis_size("blk")
    index = lax.axis_index("blk")
    core = index % 2
    side = (index // 2) % 2
    own, width, chi = edge_up.shape[1:]
    span = chi // 2
    vp = round_up(width, 8)
    per = LANES // vp
    body = width // 8 * 8
    far = []
    mask = 4
    while mask < count:
        far.append(mask)
        mask *= 2

    def swap(value, mask):
        return lax.ppermute(value, "blk", [(s, s ^ mask) for s in range(count)])

    def gather(edge):
        local = edge[0].transpose(1, 0, 2)
        keep = lax.dynamic_slice_in_dim(local, side * span, span, 2)
        give = lax.dynamic_slice_in_dim(local, (1 - side) * span, span, 2)
        have = jnp.concatenate([keep, swap(give, 2)], axis=1)
        for mask in far:
            have = jnp.concatenate([have, swap(have, mask)], axis=1)
        return jnp.concatenate([have, swap(have, 1)], axis=1)

    bits = [1] + far[::-1] + [2]

    def reorder(corner):
        value = corner[0].T
        for bit in (mask for mask in [1, 2] + far):
            pairs = value.reshape(count // (2 * bit), 2, bit, own, chi)
            value = jnp.where((index // bit) % 2 == 0, pairs, pairs[:, ::-1])
            value = value.reshape(count * own, chi)
        ways = (2,) * len(bits)
        value = value.reshape(ways + (own, chi))
        natural = sorted(bits, reverse=True)
        value = value.transpose([natural.index(bit) for bit in bits] + [len(bits), len(bits) + 1])
        return value.reshape(chi, chi).T

    def padded(rows):
        rows = jnp.pad(rows.reshape(own, width, chi), ((0, 0), (0, vp - width), (0, 0)))
        return rows.reshape(own * vp, chi)

    def with_partner(value, axis):
        return jnp.concatenate([value, swap(value, 2)], axis=axis)

    bot = gather(edge_bot)
    rows_dn = with_partner(padded(edge_dn[0]), 0)
    proj_dn_t = with_partner(padded(proj_dn[0]).T, 1)
    table_dn = make_table(site_dn[0], vp, per, body)
    grown_dn, wide_dn = make_wide(reorder(corner_dn), bot, rows_dn, vp, per)

    top = gather(edge_top)
    rows_up = with_partner(padded(edge_up[0]), 0)
    proj_up_t = with_partner(padded(proj_up[0]).T, 1)
    table_up = make_table(site_up[0], vp, per, body)

    def reduce_cut(part):
        middle = chi // 2
        keep = lax.dynamic_slice_in_dim(part, core * middle, middle, 1)
        give = lax.dynamic_slice_in_dim(part, (1 - core) * middle, middle, 1)
        total = (keep.astype(F32) + swap(give, 1).astype(F32)).astype(BF)
        for mask in far:
            total = (total.astype(F32) + swap(total, mask).astype(F32)).astype(BF)
        other = swap(total, 1)
        low = jnp.where(core == 0, total, other)
        high = jnp.where(core == 0, other, total)
        return jnp.concatenate([low, high], axis=1)

    cuts = [
        reduce_cut(make_cut(table_dn, h, wide_dn, proj_dn_t, width, vp, body)) for h in range(2)
    ]
    grown_up, wide_up = make_wide(reorder(corner_up), top, rows_up, vp, per)
    quad_up = make_quad(table_up, wide_up, width, vp, body)

    def fresh_part(grown, proj_t):
        mine = lax.dynamic_slice_in_dim(grown, index * own, own, 1)
        theirs = lax.dynamic_slice_in_dim(grown, jnp.bitwise_xor(index, 2) * own, own, 1)
        both = jnp.concatenate([mine, theirs], axis=1).reshape(width // 2, 2 * own, 2, span)
        both = both.transpose(1, 0, 2, 3).reshape(2 * own, width, span)
        both = jnp.pad(both, ((0, 0), (0, vp - width), (0, 0))).reshape(2 * own * vp, span)
        return jnp.dot(proj_t, both, preferred_element_type=F32).astype(BF)

    def spread(part):
        zero = jnp.zeros_like(part)
        return [jnp.where(side == 0, part, zero), jnp.where(side == 0, zero, part)]

    fresh = jnp.concatenate(
        spread(fresh_part(grown_up, proj_up_t)) + spread(fresh_part(grown_dn, proj_dn_t)), axis=1
    )
    fresh = lax.psum_scatter(fresh, "blk", scatter_dimension=0, tiled=True)
    columns = lax.axis_size("col")
    moved = lax.ppermute(fresh, "col", [(s, (s + 1) % columns) for s in range(columns)])

    scale = 1.0 / (chi * width) ** 0.5
    rows = own * vp
    away = make_half(quad_up, cuts, rows, rows, BF, scale)
    arrived = swap(away, 2)
    stay = make_half(quad_up, cuts, 0, rows, F32, scale)
    half = (stay + arrived.astype(F32)).astype(BF)
    half = half.reshape(own, vp, chi)[:, :width].reshape(own * width, chi)
    return (half[None], moved[None, :, :chi], moved[None, :, chi:])


def solution(mesh):
    in_specs = (
        P("col", None, None),
        P("col", None, None),
        P("col", "blk", None, None),
        P("col", "blk", None, None),
        P("col", "blk", None, None),
        P("col", "blk", None, None),
        P("col", None, None, None, None),
        P("col", None, None, None, None),
        P("col", "blk", None),
        P("col", "blk", None),
    )
    out_specs = (P("col", "blk", None), P("col", "blk", None), P("col", "blk", None))
    return jax.shard_map(
        per_device, mesh=mesh, in_specs=in_specs, out_specs=out_specs, check_vma=False
    )
```

time: 708 us -> 367 us (0.52)
  matrix products: 336 us -> 3.25 us
  local copies, waits for them, and re-layouts: 327 us -> 21 us
  Pallas kernels: 0 us -> 182 us
  waiting for transfers between devices: 20.2 us -> 105 us
  other arithmetic: 0.02 us -> 18.9 us
  starting transfers between devices: 3.41 us -> 20.1 us
    dot_general x72 -> x2, matrix products: 336 us -> 3.25 us  [fresh_part(): return jnp.dot(proj_t, both, preferred_element_type=F32).astype(BF)]
    reshape x8 -> x3, local copies, waits for them, and re-layouts: 192 us -> 1.76 us  [the longest x2 1.52 us: reorder(): return value.reshape(chi, chi).T]
    pallas_call x0 -> x9, Pallas kernels: none -> 182 us  [the longest x2 72.5 us: make_cut(): pl.pallas_call(functools.partial(cut_kernel, width, vp, body), grid=(coun...]
    ppermute x2 -> x18, waiting for transfers between devices: 0.01 us -> 105 us  [the longest x17 99.9 us: swap(): return lax.ppermute(value, 'blk', [(s, s ^ mask) for s in range(count)])]
    convert_element_type x2 -> x0, local copies, waits for them, and re-layouts: 56.7 us -> none  [enlarge(): wide = jnp.dot(edge.reshape(rows * width, chi), grown, preferred_element_...]
    transpose x2, local copies, waits for them, and re-layouts: 41.9 us -> 0.02 us  [reorder(): value.transpose([natural.index(bit) for bit in bits] + [len(bits), len(bi...]
    all_gather x2 -> x0, waiting for transfers between devices: 18.8 us -> none  [the longest x1 18.8 us: per_device(): lax.all_gather(edge_top[0], 'blk', axis=0, tiled=True)]
    ppermute x2 -> x18, starting transfers between devices: 3.07 us -> 20 us  [the longest x17 18.5 us: swap(): return lax.ppermute(value, 'blk', [(s, s ^ mask) for s in range(count)])]
  transfers between devices with their start and end apart: 6 -> 19, of which waited for: 1 -> 7; matrix products, arithmetic and copies ran while one was open for 90% -> 11% of each run, Pallas kernels for 0% -> 50%
where the time goes in v1:
time: 367 us; the launch traced here: 364 us
  Pallas kernels  182 us (50%)
  waiting for transfers between devices  105 us (29%)
  local copies, waits for them, and re-layouts  21 us (6%)
  starting transfers between devices  20.1 us (5%)
  other arithmetic  18.9 us (5%)
  between operations  14.5 us (4%)
    ppermute x17, waiting for transfers between devices, swap(): return lax.ppermute(value, 'blk', [(s, s ^ mask) for s in range(count)])  99.9 us
    pallas_call x2, Pallas kernels, make_cut(): pl.pallas_call(functools.partial(cut_kernel, width, vp, body), grid=(coun...  72.5 us
    pallas_call x1, Pallas kernels, make_quad(): pl.pallas_call(functools.partial(quad_kernel, width, vp, body), grid=(cou...  45.7 us
    pallas_call x2, Pallas kernels, make_wide(): pl.pallas_call(functools.partial(wide_kernel, vp, per, chunk), grid=(step...  31.6 us
    ppermute x17, starting transfers between devices, swap(): return lax.ppermute(value, 'blk', [(s, s ^ mask) for s in range(count)])  18.5 us
    pallas_call x2, Pallas kernels, make_table(): pl.pallas_call(functools.partial(table_kernel, width, vp, per, body), gri...  16.6 us
    pallas_call x2, Pallas kernels, make_half(): pl.pallas_call(functools.partial(half_kernel, scale), grid=(steps,), in_s...  15.2 us
  transfers between devices with their start and end apart: 19, of which 7 were waited for; matrix products, arithmetic and copies ran while one was open for 11% of the time, Pallas kernels for 50%

profile of v1, /device:TPU:0, one launch (start us, length us, event | category | flops | bytes accessed | tf_op | source)
XLA Modules:
  0.0 364.0 jit_solution(356582494977319516)
XLA Ops:
  7.3 1.9 dynamic-slice_bitcast_fusion.1
  9.1 3.0 collective-permute-start.4
  13.1 2.1 collective-permute-start.8
  15.1 1.8 dynamic-slice_bitcast_fusion.3
  17.0 1.4 copy.63
  18.5 2.1 collective-permute-start.3
  20.9 0.9 pad_maximum_fusion.10
  21.8 2.6 collective-permute-start.5
  24.5 0.8 copy.52
  25.3 0.8 copy.48
  26.0 2.0 reshape_squeeze.7
  28.0 2.0 pad.23
  30.0 8.3 %table.3.table_ref = bf16[2,648,1536]{2,1,0:T(8,128)(2,1)} custom-call(bf16[36,36,36,36]{3,2,1,0:T(8,128)(2,1)} %bitcast.78), custom_call_target="tpu_custom_call" | custom-call | bytes 30000000 | tf_op jit(solution)/shard_map/table/pallas_call | solution.py:54
  38.3 8.3 %table.2.table_ref = bf16[2,648,1536]{2,1,0:T(8,128)(2,1)} custom-call(bf16[36,36,36,36]{3,2,1,0:T(8,128)(2,1)} %bitcast.79), custom_call_target="tpu_custom_call" | custom-call | bytes 30000000 | tf_op jit(solution)/shard_map/table/pallas_call | solution.py:54
  46.6 20.7 %collective-permute-done = bf16[36,32,128]{2,1,0:T(8,128)(2,1)S(1)} collective-permute-done((bf16[36,32,128]{2,1,0:T(8,128)(2,1)}, bf16[36,32,128]{2,1,0:T(8,128)(2,1)S(1)}, u32[]{:S(2)}, u32[]{:S(2)}) %collective-permute-start) | collective-permute-done | bytes 294944 | tf_op jit(solution)/shard_map/ppermute | solution.py:263
  67.3 13.7 %collective-permute-done.5 = bf16[36,64,128]{2,1,0:T(8,128)(2,1)} collective-permute-done((bf16[36,64,128]{2,1,0:T(8,128)(2,1)}, bf16[36,64,128]{2,1,0:T(8,128)(2,1)}, u32[]{:S(2)}, u32[]{:S(2)}) %collective-permute-start.5) | collective-permute-done | bytes 589856 | tf_op jit(solution)/shard_map/ppermute | solution.py:263
  81.0 3.4 collective-permute-start.1
  84.4 1.2 pad_maximum_fusion.6
  85.6 2.3 pad_maximum_fusion.3.edge_ref
  87.9 2.3 pad_maximum_fusion.2.edge_ref
  90.2 2.2 pad_maximum_fusion.4.proj_ref
  92.4 14.0 %collective-permute-done.1 = bf16[36,64,128]{2,1,0:T(8,128)(2,1)S(1)} collective-permute-done((bf16[36,64,128]{2,1,0:T(8,128)(2,1)S(1)}, bf16[36,64,128]{2,1,0:T(8,128)(2,1)S(1)}, u32[]{:S(2)}, u32[]{:S(2)}) %collective-permute-start.1) | collective-permute-done | bytes 589856 | tf_op jit(solution)/shard_map/ppermute | solution.py:263
  106.7 2.7 pad_maximum_fusion.1.top_ref
  109.4 15.8 %wide.3 = (bf16[18,256,256]{2,1,0:T(8,128)(2,1)}, bf16[32,1536,256]{2,1,0:T(8,128)(2,1)}) custom-call(bf16[256,256]{1,0:T(8,128)(2,1)} %bitcast.108, bf16[36,256,128]{2,1,0:T(8,128)(2,1)} %pad_maximum_fusion.1.top_ref, bf16[2560,256]{1,0:T(8,128)(2,1)} %pad_maximum_fusion.3.edge_ref), custom_call_target="tpu_custom_call" | custom-call | flops 6039797760 | bytes 30000000 | tf_op jit(solution)/shard_map/wide/pallas_call | solution.py:103
  125.2 1.1 constant_dynamic-slice_fusion.1
  126.9 36.2 %cut.3 = bf16[9,256,256]{2,1,0:T(8,128)(2,1)} custom-call(bf16[2,648,1536]{2,1,0:T(8,128)(2,1)} %table.3.table_ref, bf16[32,1536,256]{2,1,0:T(8,128)(2,1)} %get-tuple-element.8.wide_ref, bf16[256,2560]{1,0:T(8,128)(2,1)} %pad_maximum_fusion.4.proj_ref), custom_call_target="tpu_custom_call" | custom-call | flops 16307453952 | bytes 30000000 | tf_op jit(solution)/shard_map/cut/pallas_call | solution.py:165
  163.2 1.1 constant_dynamic-slice_fusion.4
  164.8 36.2 %cut.2 = bf16[9,256,256]{2,1,0:T(8,128)(2,1)} custom-call(bf16[2,648,1536]{2,1,0:T(8,128)(2,1)} %table.3.table_ref, bf16[32,1536,256]{2,1,0:T(8,128)(2,1)} %get-tuple-element.8.wide_ref, bf16[256,2560]{1,0:T(8,128)(2,1)} %pad_maximum_fusion.4.proj_ref), custom_call_target="tpu_custom_call" | custom-call | flops 16307453952 | bytes 30000000 | tf_op jit(solution)/shard_map/cut/pallas_call | solution.py:165
  201.0 1.1 constant_dynamic-slice_fusion.5
  202.2 1.7 pad_maximum_fusion.top_ref
  204.0 15.8 %wide.2 = (bf16[18,256,256]{2,1,0:T(8,128)(2,1)}, bf16[32,1536,256]{2,1,0:T(8,128)(2,1)}) custom-call(bf16[256,256]{1,0:T(8,128)(2,1)} %bitcast.107, bf16[36,256,128]{2,1,0:T(8,128)(2,1)} %pad_maximum_fusion.top_ref, bf16[2560,256]{1,0:T(8,128)(2,1)} %pad_maximum_fusion.2.edge_ref), custom_call_target="tpu_custom_call" | custom-call | flops 6039797760 | bytes 30000000 | tf_op jit(solution)/shard_map/wide/pallas_call | solution.py:103
  219.7 1.1 constant_dynamic-slice_fusion.3
  221.4 1.8 broadcast_select_fusion.5
  223.2 1.3 add_convert_fusion.2
  224.6 3.5 collective-permute-start.13
  228.4 1.5 broadcast_select_fusion.7
  229.9 0.8 copy.61
  230.7 38.9 %collective-permute-done.13 = bf16[9,128,256]{2,1,0:T(8,128)(2,1)S(1)} collective-permute-done((bf16[9,128,256]{2,1,0:T(8,128)(2,1)S(1)}, bf16[9,128,256]{2,1,0:T(8,128)(2,1)S(1)}, u32[]{:S(2)}, u32[]{:S(2)}) %collective-permute-start.13) | collective-permute-done | bytes 589856 | tf_op jit(solution)/shard_map/ppermute | solution.py:263
  269.9 12.5 %collective-permute-done.10 = bf16[9,128,256]{2,1,0:T(8,128)(2,1)S(1)} collective-permute-done((bf16[9,128,256]{2,1,0:T(8,128)(2,1)S(1)}, bf16[9,128,256]{2,1,0:T(8,128)(2,1)S(1)}, u32[]{:S(2)}, u32[]{:S(2)}) %collective-permute-start.10) | collective-permute-done | bytes 589856 | tf_op jit(solution)/shard_map/ppermute | solution.py:263
  282.7 45.7 %quad.1.quad_ref = bf16[18,2560,256]{2,1,0:T(8,128)(2,1)} custom-call(bf16[2,648,1536]{2,1,0:T(8,128)(2,1)} %table.2.table_ref, bf16[32,1536,256]{2,1,0:T(8,128)(2,1)} %get-tuple-element.7.wide_ref), custom_call_target="tpu_custom_call" | custom-call | flops 32614907904 | bytes 50000000 | tf_op jit(solution)/shard_map/quad/pallas_call | solution.py:196
  328.6 1.6 pad_maximum_fusion.7
  330.1 7.6 %half.3 = bf16[1280,256]{1,0:T(8,128)(2,1)} custom-call(bf16[18,2560,256]{2,1,0:T(8,128)(2,1)} %quad.1.quad_ref, bf16[9,256,256]{2,1,0:T(8,128)(2,1)} %get-tuple-element.41.first_ref, bf16[9,256,256]{2,1,0:T(8,128)(2,1)} %get-tuple-element.42.second_ref), custom_call_target="tpu_custom_call" | custom-call | flops 3019898880 | bytes 11796480 | tf_op jit(solution)/shard_map/half/pallas_call | solution.py:228
  338.4 0.9 copy.62
  339.3 1.5 collective-permute-start.17
  340.9 4.8 %collective-permute-done.17 = bf16[32,512]{0,1:T(8,128)(2,1)S(1)} collective-permute-done((bf16[32,512]{0,1:T(8,128)(2,1)S(1)}, bf16[32,512]{0,1:T(8,128)(2,1)S(1)}, u32[]{:S(2)}, u32[]{:S(2)}) %collective-permute-start.17) | collective-permute-done | bytes 32800 | tf_op jit(solution)/shard_map/ppermute | solution.py:341
  347.0 7.7 %half.2 = f32[1280,256]{1,0:T(8,128)} custom-call(bf16[18,2560,256]{2,1,0:T(8,128)(2,1)} %quad.1.quad_ref, bf16[9,256,256]{2,1,0:T(8,128)(2,1)} %get-tuple-element.41.first_ref, bf16[9,256,256]{2,1,0:T(8,128)(2,1)} %get-tuple-element.42.second_ref), custom_call_target="tpu_custom_call" | custom-call | flops 3019898880 | bytes 11796480 | tf_op jit(solution)/shard_map/half/pallas_call | solution.py:228
  354.8 1.5 add_convert_fusion
  356.3 0.9 broadcast_in_dim_reshape.3
  (73 shorter events, 6.7 us)
Async XLA Ops:
  7.2 5.0 %copy-start.3 = (bf16[1,32,36,256]{3,1,2,0:T(8,128)(2,1)S(1)}, bf16[1,32,36,256]{3,1,2,0:T(8,128)(2,1)}, u32[]{:S(2)}) copy-start(bf16[1,32,36,256]{3,1,2,0:T(8,128)(2,1)} %param.15) | copy-start | bytes 1769476
  7.2 331.3 %reduce-scatter.4.cloned.1.call-start = ((), (), s32[]{:S(2)}) async-start(), calls=%async_computation.1 | async-start | bytes 294912
  9.1 3.5 copy-start.4
  9.1 11.8 %collective-permute-start.4 = (bf16[36,32,128]{2,1,0:T(8,128)(2,1)}, bf16[36,32,128]{2,1,0:T(8,128)(2,1)S(1)}, u32[]{:S(2)}, u32[]{:S(2)}) collective-permute-start(bf16[36,32,128]{2,1,0:T(8,128)(2,1)} %get-tuple-element.32), channel_id=1, source_target_pairs={{0,2},{1,3},{2,0},{3,1},{4,6},{5,7},{6,4},{7,5},{8,10},{9,11},{10,... | collective-permute-start | bytes 884744 | tf_op jit(solution)/shard_map/ppermute | solution.py:263
  12.5 73.0 %collective-permute-start.7 = (bf16[1280,256]{1,0:T(8,128)(2,1)S(1)}, bf16[1280,256]{1,0:T(8,128)(2,1)}, u32[]{:S(2)}, u32[]{:S(2)}) collective-permute-start(bf16[1280,256]{1,0:T(8,128)(2,1)S(1)} %bitcast.83), channel_id=1, source_target_pairs={{0,2},{1,3},{2,0},{3,1},{4,6},{5,7},{6,4},{7,5},{8,10},{9,11},{10,... | collective-permute-start | bytes 1966088 | tf_op jit(solution)/shard_map/ppermute | solution.py:263
  13.1 77.1 %collective-permute-start.8 = (bf16[256,1280]{1,0:T(8,128)(2,1)S(1)}, bf16[256,1280]{1,0:T(8,128)(2,1)}, u32[]{:S(2)}, u32[]{:S(2)}) collective-permute-start(bf16[256,1280]{1,0:T(8,128)(2,1)S(1)} %bitcast.80), channel_id=1, source_target_pairs={{0,2},{1,3},{2,0},{3,1},{4,6},{5,7},{6,4},{7,5},{8,10},{9,11},{10,... | collective-permute-start | bytes 1966088 | tf_op jit(solution)/shard_map/ppermute | solution.py:263
  16.9 3.6 copy-start.5
  16.9 50.3 %collective-permute-start = (bf16[36,32,128]{2,1,0:T(8,128)(2,1)}, bf16[36,32,128]{2,1,0:T(8,128)(2,1)S(1)}, u32[]{:S(2)}, u32[]{:S(2)}) collective-permute-start(bf16[36,32,128]{2,1,0:T(8,128)(2,1)} %get-tuple-element.34), channel_id=1, source_target_pairs={{0,2},{1,3},{2,0},{3,1},{4,6},{5,7},{6,4},{7,5},{8,10},{9,11},{10,... | collective-permute-start | bytes 884744 | tf_op jit(solution)/shard_map/ppermute | solution.py:263
  17.0 3.7 %copy-start.6 = (bf16[1,256,256]{2,1,0:T(8,128)(2,1)S(1)}, bf16[1,256,256]{2,1,0:T(8,128)(2,1)}, u32[]{:S(2)}) copy-start(bf16[1,256,256]{2,1,0:T(8,128)(2,1)} %param.10) | copy-start | bytes 393220
  18.5 69.4 %collective-permute-start.3 = (bf16[1280,256]{1,0:T(8,128)(2,1)S(1)}, bf16[1280,256]{1,0:T(8,128)(2,1)}, u32[]{:S(2)}, u32[]{:S(2)}) collective-permute-start(bf16[1280,256]{1,0:T(8,128)(2,1)S(1)} %bitcast.85), channel_id=1, source_target_pairs={{0,2},{1,3},{2,0},{3,1},{4,6},{5,7},{6,4},{7,5},{8,10},{9,11},{10,... | collective-permute-start | bytes 1966088 | tf_op jit(solution)/shard_map/ppermute | solution.py:263
  21.8 59.2 %collective-permute-start.5 = (bf16[36,64,128]{2,1,0:T(8,128)(2,1)}, bf16[36,64,128]{2,1,0:T(8,128)(2,1)}, u32[]{:S(2)}, u32[]{:S(2)}) collective-permute-start(bf16[36,64,128]{2,1,0:T(8,128)(2,1)} %pad_maximum_fusion.10), channel_id=1, source_target_pairs={{0,4},{1,5},{2,6},{3,7},{4,0},{5,1},{6,2},{7,3},{8,12},{9,13},{10,... | collective-permute-start | bytes 1769480 | tf_op jit(solution)/shard_map/ppermute | solution.py:263
  67.2 161.1 %collective-permute-start.16 = (bf16[256,1280]{0,1:T(8,128)(2,1)}, bf16[256,1280]{0,1:T(8,128)(2,1)}, u32[]{:S(2)}, u32[]{:S(2)}) collective-permute-start(bf16[256,1280]{0,1:T(8,128)(2,1)} %bitcast.91), channel_id=1, source_target_pairs={{0,2},{1,3},{2,0},{3,1},{4,6},{5,7},{6,4},{7,5},{8,10},{9,11},{10,... | collective-permute-start | bytes 1966088 | tf_op jit(solution)/shard_map/ppermute | solution.py:263
  81.0 25.5 %collective-permute-start.1 = (bf16[36,64,128]{2,1,0:T(8,128)(2,1)S(1)}, bf16[36,64,128]{2,1,0:T(8,128)(2,1)S(1)}, u32[]{:S(2)}, u32[]{:S(2)}) collective-permute-start(bf16[36,64,128]{2,1,0:T(8,128)(2,1)S(1)} %pad_maximum_fusion.9), channel_id=1, source_target_pairs={{0,4},{1,5},{2,6},{3,7},{4,0},{5,1},{6,2},{7,3},{8,12},{9,13},{10,... | collective-permute-start | bytes 1769480 | tf_op jit(solution)/shard_map/ppermute | solution.py:263
  85.6 21.1 %collective-permute-start.6 = (bf16[36,128,128]{2,1,0:T(8,128)(2,1)S(1)}, bf16[36,128,128]{2,1,0:T(8,128)(2,1)S(1)}, u32[]{:S(2)}, u32[]{:S(2)}) collective-permute-start(bf16[36,128,128]{2,1,0:T(8,128)(2,1)S(1)} %pad_maximum_fusion.6), channel_id=1, source_target_pairs={{0,1},{1,0},{2,3},{3,2},{4,5},{5,4},{6,7},{7,6},{8,9},{9,8},{10,11... | collective-permute-start | bytes 3538952 | tf_op jit(solution)/shard_map/ppermute | solution.py:263
  106.6 95.7 %collective-permute-start.2 = (bf16[36,128,128]{2,1,0:T(8,128)(2,1)S(1)}, bf16[36,128,128]{2,1,0:T(8,128)(2,1)S(1)}, u32[]{:S(2)}, u32[]{:S(2)}) collective-permute-start(bf16[36,128,128]{2,1,0:T(8,128)(2,1)S(1)} %pad_maximum_fusion.5), channel_id=1, source_target_pairs={{0,1},{1,0},{2,3},{3,2},{4,5},{5,4},{6,7},{7,6},{8,9},{9,8},{10,11... | collective-permute-start | bytes 3538952 | tf_op jit(solution)/shard_map/ppermute | solution.py:263
  164.3 58.9 %collective-permute-start.12 = (bf16[9,128,256]{2,1,0:T(8,128)(2,1)S(1)}, bf16[9,128,256]{2,1,0:T(8,128)(2,1)}, u32[]{:S(2)}, u32[]{:S(2)}) collective-permute-start(bf16[9,128,256]{2,1,0:T(8,128)(2,1)S(1)} %constant_dynamic-slice_fusion.4), channel_id=1, source_target_pairs={{0,1},{1,0},{2,3},{3,2},{4,5},{5,4},{6,7},{7,6},{8,9},{9,8},{10,11... | collective-permute-start | bytes 1769480 | tf_op jit(solution)/shard_map/ppermute | solution.py:263
  202.1 25.9 %collective-permute-start.9 = (bf16[9,128,256]{2,1,0:T(8,128)(2,1)S(1)}, bf16[9,128,256]{2,1,0:T(8,128)(2,1)S(1)}, u32[]{:S(2)}, u32[]{:S(2)}) collective-permute-start(bf16[9,128,256]{2,1,0:T(8,128)(2,1)S(1)} %constant_dynamic-slice_fusion.5), channel_id=1, source_target_pairs={{0,1},{1,0},{2,3},{3,2},{4,5},{5,4},{6,7},{7,6},{8,9},{9,8},{10,11... | collective-permute-start | bytes 1769480 | tf_op jit(solution)/shard_map/ppermute | solution.py:263
  221.4 1.8 copy-start.1
  223.2 4.9 %copy-start = (bf16[9,256,256]{2,1,0:T(8,128)(2,1)S(1)}, bf16[9,256,256]{2,1,0:T(8,128)(2,1)}, u32[]{:S(2)}) copy-start(bf16[9,256,256]{2,1,0:T(8,128)(2,1)} %cut.2) | copy-start | bytes 3538948
  224.6 3.8 %copy-start.2 = (bf16[32,40,256]{2,1,0:T(8,128)(2,1)S(1)}, bf16[32,40,256]{2,1,0:T(8,128)(2,1)}, u32[]{:S(2)}) copy-start(bf16[32,40,256]{2,1,0:T(8,128)(2,1)} %pad.23) | copy-start | bytes 1966084
  224.6 45.1 %collective-permute-start.13 = (bf16[9,128,256]{2,1,0:T(8,128)(2,1)S(1)}, bf16[9,128,256]{2,1,0:T(8,128)(2,1)S(1)}, u32[]{:S(2)}, u32[]{:S(2)}) collective-permute-start(bf16[9,128,256]{2,1,0:T(8,128)(2,1)S(1)} %add_convert_fusion.2), channel_id=1, source_target_pairs={{0,4},{1,5},{2,6},{3,7},{4,0},{5,1},{6,2},{7,3},{8,12},{9,13},{10,... | collective-permute-start | bytes 1769480 | tf_op jit(solution)/shard_map/ppermute | solution.py:263
  228.2 54.2 %collective-permute-start.10 = (bf16[9,128,256]{2,1,0:T(8,128)(2,1)S(1)}, bf16[9,128,256]{2,1,0:T(8,128)(2,1)S(1)}, u32[]{:S(2)}, u32[]{:S(2)}) collective-permute-start(bf16[9,128,256]{2,1,0:T(8,128)(2,1)S(1)} %add_convert_fusion.4), channel_id=1, source_target_pairs={{0,4},{1,5},{2,6},{3,7},{4,0},{5,1},{6,2},{7,3},{8,12},{9,13},{10,... | collective-permute-start | bytes 1769480 | tf_op jit(solution)/shard_map/ppermute | solution.py:263
  269.8 58.5 %collective-permute-start.14 = (bf16[9,128,256]{2,1,0:T(8,128)(2,1)S(1)}, bf16[9,128,256]{2,1,0:T(8,128)(2,1)S(1)}, u32[]{:S(2)}, u32[]{:S(2)}) collective-permute-start(bf16[9,128,256]{2,1,0:T(8,128)(2,1)S(1)} %add_convert_fusion.1), channel_id=1, source_target_pairs={{0,1},{1,0},{2,3},{3,2},{4,5},{5,4},{6,7},{7,6},{8,9},{9,8},{10,11... | collective-permute-start | bytes 1769480 | tf_op jit(solution)/shard_map/ppermute | solution.py:263
  282.6 45.9 %collective-permute-start.11 = (bf16[9,128,256]{2,1,0:T(8,128)(2,1)S(1)}, bf16[9,128,256]{2,1,0:T(8,128)(2,1)S(1)}, u32[]{:S(2)}, u32[]{:S(2)}) collective-permute-start(bf16[9,128,256]{2,1,0:T(8,128)(2,1)S(1)} %add_convert_fusion.3), channel_id=1, source_target_pairs={{0,1},{1,0},{2,3},{3,2},{4,5},{5,4},{6,7},{7,6},{8,9},{9,8},{10,11... | collective-permute-start | bytes 1769480 | tf_op jit(solution)/shard_map/ppermute | solution.py:263
  337.7 17.1 %collective-permute-start.15 = (bf16[1280,256]{1,0:T(8,128)(2,1)}, bf16[1280,256]{1,0:T(8,128)(2,1)S(1)}, u32[]{:S(2)}, u32[]{:S(2)}) collective-permute-start(bf16[1280,256]{1,0:T(8,128)(2,1)} %half.3), channel_id=1, source_target_pairs={{0,2},{1,3},{2,0},{3,1},{4,6},{5,7},{6,4},{7,5},{8,10},{9,11},{10,... | collective-permute-start | bytes 1966088 | tf_op jit(solution)/shard_map/ppermute | solution.py:263
  339.3 6.3 %collective-permute-start.17 = (bf16[32,512]{0,1:T(8,128)(2,1)S(1)}, bf16[32,512]{0,1:T(8,128)(2,1)S(1)}, u32[]{:S(2)}, u32[]{:S(2)}) collective-permute-start(bf16[32,512]{0,1:T(8,128)(2,1)S(1)} %copy.62), channel_id=1, source_target_pairs={{0,8},{8,16},{16,24},{24,0},{1,9},{9,17},{17,25},{25,1},{2,10},{10... | collective-permute-start | bytes 98312 | tf_op jit(solution)/shard_map/ppermute | solution.py:341
Sparse Core Ops, SparseCore 0:
  230.9 41.0 reduce-scatter.3
